TPU v7x, 128 devices: a whole 4x4x4 slice. The times are simulated.
128 devices in a mesh: dp: 32 (over z, x, core), fs: 4 (over y).
Axes of the slice: x: 4, y: 4, z: 4, core: 2. Of those that a mesh axis runs over, the one named last changes fastest.
Arguments:
- tokens: bfloat16 [12288, 3584], P('dp', 'fs'), may hold values from -12 to 12
- cotangent: bfloat16 [12288, 3584], P('dp', 'fs'), may hold values from -6 to 6
- w_query: bfloat16 [3584, 3584], P('dp', 'fs'), may hold values from -0.09375 to 0.09375
- w_key: bfloat16 [3584, 512], P('dp', 'fs'), may hold values from -0.09375 to 0.09375
- w_value: bfloat16 [3584, 512], P('dp', 'fs'), may hold values from -0.09375 to 0.09375
- w_out: bfloat16 [3584, 3584], P('fs', 'dp'), may hold values from -0.09375 to 0.09375
- route: int32 [12288], replicated, may hold values from 0 to 12287, as said below
- doc_lengths: int32 [32, 2], P('dp'), may hold values from 1 to 288, 384 in all within a row
Outputs:
- out_home: bfloat16 [12288, 3584], P('dp', 'fs')
- grad_in: bfloat16 [12288, 3584], P('dp', 'fs')
- grad_wq: bfloat16 [3584, 3584], P('dp', 'fs')
- grad_wk: bfloat16 [3584, 512], P('dp', 'fs')
- grad_wv: bfloat16 [3584, 512], P('dp', 'fs')
- grad_wo: bfloat16 [3584, 3584], P('fs', 'dp')
Inputs may be any that keep to these rules, and one draw needn't show every extreme that they name: route is a permutation; home block i sends exactly 384 // 32 rows to each planned block. `doc_lengths`: each row holds two responses whose lengths sum to 384.
All inputs are finite; a program needn't handle non-finite values.
Results may differ from a plain program's by a relative error of at most 0.025.
Values may be sent and summed in bfloat16 or wider, within the bound.
No kernel may reach another device: no remote copies, remote signals or barrier semaphores. Data moves between devices by JAX's collectives and lax.ppermute only.
A program may use at most 128 MiB of HBM per device.

v0:
```python
import jax
import jax.numpy as jnp
from jax import lax
from jax.sharding import PartitionSpec as P

HS = 128


theta_base = 1000000.0


def doc_layout(lengths, count_rows):
    ends = jnp.cumsum(lengths)
    starts = ends - lengths
    rows = jnp.arange(count_rows, dtype=jnp.int32)
    doc_of = jnp.sum((rows[:, None] >= ends[None, :]).astype(jnp.int32), axis=1)
    which = doc_of[:, None] == jnp.arange(lengths.shape[0], dtype=jnp.int32)[None, :]
    start_of = jnp.sum(jnp.where(which, starts[None, :], 0), axis=1)
    position = rows - start_of
    allowed = (doc_of[:, None] == doc_of[None, :]) & (rows[None, :] <= rows[:, None])
    return (position, allowed)


def angles(position, width):
    freq = theta_base ** (-(jnp.arange(width // 2, dtype=jnp.float32) * 2.0) / width)
    phase = position.astype(jnp.float32)[:, None] * freq[None, :]
    return (jnp.cos(phase), jnp.sin(phase))


def rotate(values, cosine, sine):
    half = values.shape[-1] // 2
    first = values[..., :half]
    second = values[..., half:]
    cos_b = cosine[:, None, :]
    sin_b = sine[:, None, :]
    return jnp.concatenate(
        [first * cos_b - second * sin_b, second * cos_b + first * sin_b], axis=-1
    )


def unrotate(grads, cosine, sine):
    half = grads.shape[-1] // 2
    first = grads[..., :half]
    second = grads[..., half:]
    cos_b = cosine[:, None, :]
    sin_b = sine[:, None, :]
    return jnp.concatenate(
        [first * cos_b + second * sin_b, second * cos_b - first * sin_b], axis=-1
    )


def attend_forward(query, keys, values, allowed, scale):
    scores = jnp.einsum("qcgd,kcd->cgqk", query, keys, preferred_element_type=jnp.float32) * scale
    scores = jnp.where(allowed[None, None], scores, -1e30)
    top = jnp.max(scores, axis=-1, keepdims=True)
    expo = jnp.exp(scores - top)
    probs = expo / jnp.sum(expo, axis=-1, keepdims=True)
    probs_low = probs.astype(jnp.bfloat16)
    attended = jnp.einsum("cgqk,kcd->qcgd", probs_low, values, preferred_element_type=jnp.float32)
    return (attended.astype(jnp.bfloat16), probs, probs_low)


def attend_backward(query, keys, values, attended, d_att, probs, probs_low, scale):
    d_probs = jnp.einsum("qcgd,kcd->cgqk", d_att, values, preferred_element_type=jnp.float32)
    delta = jnp.einsum("qcgd,qcgd->cgq", d_att, attended, preferred_element_type=jnp.float32)
    d_scores = (probs * (d_probs - delta[..., None]) * scale).astype(jnp.bfloat16)
    d_query = jnp.einsum("cgqk,kcd->qcgd", d_scores, keys, preferred_element_type=jnp.float32)
    d_keys = jnp.einsum("cgqk,qcgd->kcd", d_scores, query, preferred_element_type=jnp.float32)
    d_values = jnp.einsum("cgqk,qcgd->kcd", probs_low, d_att, preferred_element_type=jnp.float32)
    return (d_query, d_keys, d_values.astype(jnp.bfloat16))


def contract_rows(left, right):
    return lax.dot_general(
        left, right, (((0,), (0,)), ((), ())), preferred_element_type=jnp.float32
    )


def contract_cols(left, right):
    return lax.dot_general(
        left, right, (((1,), (1,)), ((), ())), preferred_element_type=jnp.float32
    )


def local(tokens, cotangent, w_query, w_key, w_value, w_out, route, doc_lengths):
    count_dp = lax.axis_size("dp")
    my_index = lax.axis_index("dp")
    count_rows = tokens.shape[0]
    piece_rows = count_rows // count_dp
    scale = HS ** (-0.5)
    line_ids = jnp.arange(count_rows, dtype=jnp.int32)
    own_route = lax.dynamic_slice_in_dim(route, my_index * count_rows, count_rows)
    send_rank = jnp.sum((own_route[None, :] < own_route[:, None]).astype(jnp.int32), axis=1)
    send_table = (send_rank[None, :] == line_ids[:, None]).astype(jnp.bfloat16)
    inverse = (
        jnp.zeros(route.shape, jnp.int32).at[route].set(jnp.arange(route.shape[0], dtype=jnp.int32))
    )
    home_rows = lax.dynamic_slice_in_dim(inverse, my_index * count_rows, count_rows)
    source = home_rows // count_rows
    earlier = (source[None, :] == source[:, None]) & (line_ids[None, :] < line_ids[:, None])
    buffer_row = source * piece_rows + jnp.sum(earlier.astype(jnp.int32), axis=1)
    recv_table = (buffer_row[:, None] == line_ids[None, :]).astype(jnp.bfloat16)

    def outbound(values):
        moved = jnp.dot(send_table, values, preferred_element_type=jnp.float32).astype(jnp.bfloat16)
        return moved.reshape(count_dp, piece_rows, values.shape[1])

    def inbound(values):
        flat_in = values.reshape(count_rows, values.shape[2])
        return jnp.dot(recv_table, flat_in, preferred_element_type=jnp.float32).astype(jnp.bfloat16)

    x_recv = lax.all_to_all(outbound(tokens), "dp", split_axis=0, concat_axis=0, tiled=True)
    x_full = lax.all_gather(inbound(x_recv), "fs", axis=1, tiled=True)
    wq_full, wk_full, wv_full, wo_full = (
        lax.all_gather(w_query, "dp", axis=0, tiled=True),
        lax.all_gather(w_key, "dp", axis=0, tiled=True),
        lax.all_gather(w_value, "dp", axis=0, tiled=True),
        lax.all_gather(w_out, "dp", axis=1, tiled=True),
    )
    heads_here = wq_full.shape[1] // HS
    kv_here = wk_full.shape[1] // HS
    groups = heads_here // kv_here
    position, allowed = doc_layout(doc_lengths[0], count_rows)
    cosine, sine = angles(position, HS)
    q_pre = jnp.dot(x_full, wq_full, preferred_element_type=jnp.float32).reshape(
        count_rows, heads_here, HS
    )
    query = (
        rotate(q_pre, cosine, sine).astype(jnp.bfloat16).reshape(count_rows, kv_here, groups, HS)
    )
    k_pre = jnp.dot(x_full, wk_full, preferred_element_type=jnp.float32).reshape(
        count_rows, kv_here, HS
    )
    keys = rotate(k_pre, cosine, sine).astype(jnp.bfloat16)
    values = (
        jnp.dot(x_full, wv_full, preferred_element_type=jnp.float32)
        .astype(jnp.bfloat16)
        .reshape(count_rows, kv_here, HS)
    )
    attended, probs, probs_low = attend_forward(query, keys, values, allowed, scale)
    flat = attended.reshape(count_rows, heads_here * HS)
    head_part = jnp.dot(flat, wo_full, preferred_element_type=jnp.float32)
    out_planned = lax.psum_scatter(
        head_part.astype(jnp.bfloat16), "fs", scatter_dimension=1, tiled=True
    )
    going_home = jnp.dot(recv_table.T, out_planned, preferred_element_type=jnp.float32).astype(
        jnp.bfloat16
    )
    returned = lax.all_to_all(
        going_home.reshape(count_dp, piece_rows, out_planned.shape[1]),
        "dp",
        split_axis=0,
        concat_axis=0,
        tiled=True,
    )
    returned = returned.reshape(count_rows, out_planned.shape[1])
    out_home = jnp.dot(send_table.T, returned, preferred_element_type=jnp.float32).astype(
        jnp.bfloat16
    )
    c_recv = lax.all_to_all(outbound(cotangent), "dp", split_axis=0, concat_axis=0, tiled=True)
    c_full = lax.all_gather(inbound(c_recv), "fs", axis=1, tiled=True)
    d_att = (
        contract_cols(c_full, wo_full).astype(jnp.bfloat16).reshape(count_rows, kv_here, groups, HS)
    )
    grad_out_part = contract_rows(flat, c_full)
    d_query, d_keys, d_values = attend_backward(
        query, keys, values, attended, d_att, probs, probs_low, scale
    )
    dq_flat = unrotate(d_query.reshape(count_rows, heads_here, HS), cosine, sine).astype(
        jnp.bfloat16
    )
    dq_flat = dq_flat.reshape(count_rows, heads_here * HS)
    dk_flat = unrotate(d_keys, cosine, sine).astype(jnp.bfloat16).reshape(count_rows, kv_here * HS)
    dv_flat = d_values.reshape(count_rows, kv_here * HS)
    grad_rows = (
        contract_cols(dq_flat, wq_full)
        + contract_cols(dk_flat, wk_full)
        + contract_cols(dv_flat, wv_full)
    )
    grad_in = lax.psum_scatter(
        grad_rows.astype(jnp.bfloat16), "fs", scatter_dimension=1, tiled=True
    )
    grad_q_part = contract_rows(x_full, dq_flat)
    grad_k_part = contract_rows(x_full, dk_flat)
    grad_v_part = contract_rows(x_full, dv_flat)
    q_sum, k_sum, v_sum, wo_sum = (
        lax.psum_scatter(
            grad_q_part.astype(jnp.bfloat16), "dp", scatter_dimension=0, tiled=True
        ).astype(jnp.float32),
        lax.psum_scatter(
            grad_k_part.astype(jnp.bfloat16), "dp", scatter_dimension=0, tiled=True
        ).astype(jnp.float32),
        lax.psum_scatter(
            grad_v_part.astype(jnp.bfloat16), "dp", scatter_dimension=0, tiled=True
        ).astype(jnp.float32),
        lax.psum_scatter(
            grad_out_part.astype(jnp.bfloat16), "dp", scatter_dimension=1, tiled=True
        ).astype(jnp.float32),
    )
    return (
        out_home,
        grad_in,
        q_sum.astype(jnp.bfloat16),
        k_sum.astype(jnp.bfloat16),
        v_sum.astype(jnp.bfloat16),
        wo_sum.astype(jnp.bfloat16),
    )


def solution(mesh):
    in_specs = (
        P("dp", "fs"),
        P("dp", "fs"),
        P("dp", "fs"),
        P("dp", "fs"),
        P("dp", "fs"),
        P("fs", "dp"),
        P(),
        P("dp", None),
    )
    out_specs = (
        P("dp", "fs"),
        P("dp", "fs"),
        P("dp", "fs"),
        P("dp", "fs"),
        P("dp", "fs"),
        P("fs", "dp"),
    )
    return jax.shard_map(local, mesh=mesh, in_specs=in_specs, out_specs=out_specs, check_vma=False)
```

profile of v0, /device:TPU:0, one launch (start us, length us, event | category | flops | bytes accessed | tf_op | source)
XLA Modules:
  0.0 690.9 jit_solution(1593534024469527159)
XLA Ops:
  7.2 0.8 dynamic_slice.6
  8.3 0.5 convolution_convert_fusion.11
  8.8 1.1 reshape.307
  9.9 8.4 %all-to-all-start = ((bf16[32,12,896]{2,1,0:T(8,128)(2,1)}), bf16[32,12,896]{2,1,0:T(8,128)(2,1)S(1)}, u32[]{:S(2)}, u32[]{:S(2)}) async-start(bf16[32,12,896]{2,1,0:T(8,128)(2,1)} %reshape.307), calls=%async_computation | async-start | bytes 1835008 | tf_op jit(solution)/shard_map/all_to_all | solution.py:112
  18.4 45.4 %scatter_custom_fusion = s32[12288]{0:T(1024)S(1)} fusion(s32[12288]{0:T(1024)S(1)} %compare_select_fusion, s32[12288]{0:T(1024)S(1)} %iota.36, s32[]{:T(128)} %constant.10.clone.1), kind=kCustom, calls=%fused_computation.94 | custom fusion | bytes 49156 | tf_op jit(solution)/shard_map/scatter | solution.py:96
  64.4 1.4 convolution_convert_fusion.10
  65.9 0.7 all-gather.7.cloned.1.call-update
  66.7 0.5 convolution_convert_fusion.7
  67.4 23.1 %all_to_all.15 = bf16[32,12,896]{2,1,0:T(8,128)(2,1)S(1)} all-to-all(bf16[32,12,896]{2,1,0:T(8,128)(2,1)S(1)} %reshape.317), channel_id=1, replica_groups=mesh['dp'=32,'fs'=4] {'dp'}, dimensions={0} | all-to-all | bytes 1376256 | tf_op jit(solution)/shard_map/all_to_all | solution.py:160
  90.7 1.4 convolution_convert_fusion.6
  92.2 0.5 all-gather.9.cloned.1.call-update
  93.1 24.9 %all_gather.20 = bf16[3584,128]{1,0:T(8,128)(2,1)} all-gather(bf16[112,128]{1,0:T(8,128)(2,1)S(1)} %copy-done.24), channel_id=1, replica_groups=mesh['dp'=32,'fs'=4] {'dp'}, dimensions={0}, use_global_device_ids=true | all-gather | bytes 946176 | tf_op jit(solution)/shard_map/all_gather | solution.py:116
  118.1 27.2 %all_gather.19 = bf16[3584,128]{1,0:T(8,128)(2,1)} all-gather(bf16[112,128]{1,0:T(8,128)(2,1)S(1)} %copy-done.25), channel_id=1, replica_groups=mesh['dp'=32,'fs'=4] {'dp'}, dimensions={0}, use_global_device_ids=true | all-gather | bytes 946176 | tf_op jit(solution)/shard_map/all_gather | solution.py:117
  145.3 0.8 fusion.38
  146.0 1.5 multiply_cosine_fusion
  147.5 3.2 convolution_bitcast_fusion
  150.8 0.4 fusion.65
  151.3 1.5 fusion.32
  152.8 3.4 all-gather.7.cloned.1.call-done
  156.2 6.1 fusion.80
  162.4 1.0 fusion.79
  163.3 2.7 copy.93
  166.0 1.5 copy.94
  167.5 26.1 %all-gather.11.cloned.1.call-done = bf16[384,3584]{1,0:T(8,128)(2,1)} async-done(((bf16[384,896]{1,0:T(8,128)(2,1)}), bf16[384,3584]{1,0:T(8,128)(2,1)}) %all-gather.11.cloned.1.call-update) | async-done | bytes 2752528 | tf_op jit(solution)/shard_map/all_gather | solution.py:161
  193.6 51.8 %all-gather.9.cloned.1.call-done = bf16[896,3584]{0,1:T(8,128)(2,1)} async-done(((bf16[896,112]{0,1:T(8,128)(2,1)}), bf16[896,3584]{0,1:T(8,128)(2,1)}) %all-gather.9.cloned.1.call-update) | async-done | bytes 6422544 | tf_op jit(solution)/shard_map/all_gather | solution.py:118
  245.4 6.7 convolution_convert_fusion.5
  252.0 1.1 copy.60
  253.2 2.2 subtract_convert_fusion.1
  255.4 1.2 fusion.6
  256.7 0.9 fusion.5
  257.6 0.7 copy-done.15
  258.3 2.0 fusion.19
  260.3 0.9 copy-done.32
  261.3 4.4 convolution_convert_fusion.2
  265.7 4.5 copy.88
  270.4 4.0 fusion.3
  274.5 1.0 fusion.16
  276.0 0.5 add_convert_fusion
  276.5 1.2 pad_maximum_fusion.1
  277.8 2.3 copy.64
  280.1 3.0 fusion.26
  283.1 0.4 fusion.63
  283.6 5.3 fusion.81
  289.0 0.9 convolution_add_fusion.1
  289.9 1.3 copy-done.4
  291.4 1.3 fusion.33
  292.7 2.4 fusion
  295.1 4.5 copy.90
  299.7 1.9 convolution_convert_fusion.4
  301.6 1.9 convolution_convert_fusion.3
  303.8 5.8 convolution_convert_fusion.1
  309.7 1.7 copy-done.30
  311.5 5.8 convolution_convert_fusion
  317.3 0.6 copy-done.21
  318.0 2.0 convolution_convert_fusion.9
  320.0 1.1 reshape.315
  321.1 4.9 all-to-all-start.1
  325.9 15.3 %reduce-scatter.21.cloned.1.call-done = bf16[896,384]{1,0:T(8,128)(2,1)} async-done(((bf16[3584,384]{1,0:T(8,128)(2,1)}), bf16[896,384]{1,0:T(8,128)(2,1)}) %reduce-scatter.21.cloned.1.call-update) | async-done | bytes 688144
  341.2 2.2 copy.91
  343.6 1.5 convolution_convert_fusion.8
  345.1 75.2 %reduce-scatter.13.cloned.1.call-done = bf16[112,128]{1,0:T(8,128)(2,1)} async-done(((bf16[3584,128]{1,0:T(8,128)(2,1)}), bf16[112,128]{1,0:T(8,128)(2,1)}) %reduce-scatter.13.cloned.1.call-update) | async-done | bytes 28688 | tf_op jit(solution)/shard_map/reduce_scatter | solution.py:190
  420.3 78.5 %reduce-scatter.15.cloned.1.call-done = bf16[112,128]{1,0:T(8,128)(2,1)} async-done(((bf16[3584,128]{1,0:T(8,128)(2,1)}), bf16[112,128]{1,0:T(8,128)(2,1)}) %reduce-scatter.15.cloned.1.call-update) | async-done | bytes 28688 | tf_op jit(solution)/shard_map/reduce_scatter | solution.py:193
  498.8 92.6 %reduce-scatter.11.cloned.1.call-done = bf16[112,896]{1,0:T(8,128)(2,1)} async-done(((bf16[3584,896]{1,0:T(8,128)(2,1)}), bf16[112,896]{1,0:T(8,128)(2,1)}) %reduce-scatter.11.cloned.1.call-update) | async-done | bytes 200720 | tf_op jit(solution)/shard_map/reduce_scatter | solution.py:187
  591.4 92.4 %reduce-scatter.17.cloned.1.call-done = bf16[896,112]{0,1:T(8,128)(2,1)} async-done(((bf16[896,3584]{0,1:T(8,128)(2,1)}), bf16[896,112]{0,1:T(8,128)(2,1)}) %reduce-scatter.17.cloned.1.call-update) | async-done | bytes 200720 | tf_op jit(solution)/shard_map/reduce_scatter | solution.py:196
  (108 shorter events, 3.7 us)
Async XLA Ops:
  7.2 1.1 copy-start
  7.2 11.2 %copy-start.19 = (s32[12288]{0:T(1024)S(1)}, s32[12288]{0:T(1024)}, u32[]{:S(2)}) copy-start(s32[12288]{0:T(1024)} %param.14) | copy-start | bytes 147460
  9.9 56.8 %copy-start.14 = (bf16[384,896]{1,0:T(8,128)(2,1)S(1)}, bf16[384,896]{1,0:T(8,128)(2,1)}, u32[]{:S(2)}) copy-start(bf16[384,896]{1,0:T(8,128)(2,1)} %param.9) | copy-start | bytes 2064388
  9.9 54.3 %all-to-all-start = ((bf16[32,12,896]{2,1,0:T(8,128)(2,1)}), bf16[32,12,896]{2,1,0:T(8,128)(2,1)S(1)}, u32[]{:S(2)}, u32[]{:S(2)}) async-start(bf16[32,12,896]{2,1,0:T(8,128)(2,1)} %reshape.307), calls=%async_computation | async-start | bytes 1835008 | tf_op jit(solution)/shard_map/all_to_all | solution.py:112
  18.3 129.2 %all-gather.5.cloned.1.call-start = ((), (), s32[]{:S(2)}) async-start(), calls=%async_computation.9 | async-start | bytes 3440640 | tf_op jit(solution)/shard_map/all_gather | solution.py:113
  64.2 26.4 %copy-start.20 = (s32[384]{0:T(512)}, s32[384]{0:T(512)S(1)}, u32[]{:S(2)}) copy-start(s32[384]{0:T(512)S(1)} %multiply_add_fusion) | copy-start | bytes 4612
  65.9 90.4 %all-gather.7.cloned.1.call-start = ((), (), s32[]{:S(2)}) async-start(), calls=%async_computation.10 | async-start | bytes 6623232 | tf_op jit(solution)/shard_map/all_gather | solution.py:115
  66.6 126.9 %all-gather.11.cloned.1.call-start = ((), (), s32[]{:S(2)}) async-start(), calls=%async_computation.12 | async-start | bytes 3440640 | tf_op jit(solution)/shard_map/all_gather | solution.py:161
  67.4 25.4 %copy-start.31 = (s32[1,2]{1,0:T(1,128)S(1)}, s32[1,2]{1,0:T(1,128)}, u32[]{:S(2)}) copy-start(s32[1,2]{1,0:T(1,128)} %param.15) | copy-start | bytes 28
  67.4 25.8 %copy-start.24 = (bf16[112,128]{1,0:T(8,128)(2,1)S(1)}, bf16[112,128]{1,0:T(8,128)(2,1)}, u32[]{:S(2)}) copy-start(bf16[112,128]{1,0:T(8,128)(2,1)} %param.11) | copy-start | bytes 86020
  90.5 27.5 %copy-start.25 = (bf16[112,128]{1,0:T(8,128)(2,1)S(1)}, bf16[112,128]{1,0:T(8,128)(2,1)}, u32[]{:S(2)}) copy-start(bf16[112,128]{1,0:T(8,128)(2,1)} %param.12) | copy-start | bytes 86020
  92.1 153.2 %all-gather.9.cloned.1.call-start = ((), (), s32[]{:S(2)}) async-start(), calls=%async_computation.11 | async-start | bytes 6623232 | tf_op jit(solution)/shard_map/all_gather | solution.py:118
  92.7 224.6 %reduce-scatter.19.cloned.1.call-start = ((), (), s32[]{:S(2)}) async-start(), calls=%async_computation.17 | async-start | bytes 3440640
  93.0 57.8 %copy-start.28 = (f32[64]{0:T(128)}, f32[64]{0:T(128)S(1)}, u32[]{:S(2)}) copy-start(f32[64]{0:T(128)S(1)} %multiply_power_fusion) | copy-start | bytes 772
  145.2 7.5 %copy-start.22 = (f32[384]{0:T(512)}, f32[384]{0:T(512)S(1)}, u32[]{:S(2)}) copy-start(f32[384]{0:T(512)S(1)} %subtract_convert_fusion.2) | copy-start | bytes 4612
  147.5 3.7 copy-start.2
  147.5 3.7 copy-start.8
  253.2 2.2 copy-start.12
  255.4 1.2 copy-start.7
  256.6 3.7 copy-start.3
  256.6 1.6 copy-start.15
  256.6 1.7 copy-start.34
  256.7 4.6 slice-start
  257.5 2.8 copy-start.26
  258.3 3.0 slice-start.1
  260.3 0.9 copy-start.32
  270.2 71.0 %reduce-scatter.21.cloned.1.call-start = ((), (), s32[]{:S(2)}) async-start(), calls=%async_computation.18 | async-start | bytes 3440640
  274.5 2.0 copy-start.5
  274.5 1.1 copy-start.10
  274.5 1.5 copy-start.11
  277.8 5.3 copy-start.23
  277.8 5.3 copy-start.29
  280.1 3.4 copy-start.17
  283.6 5.3 copy-start.6
  288.9 2.2 copy-start.4
  288.9 2.2 copy-start.13
  288.9 2.4 copy-start.16
  288.9 2.4 copy-start.27
  291.4 1.3 copy-start.9
  299.6 120.6 %reduce-scatter.13.cloned.1.call-start = ((), (), s32[]{:S(2)}) async-start(), calls=%async_computation.14 | async-start | bytes 946176 | tf_op jit(solution)/shard_map/reduce_scatter | solution.py:190
  301.6 2.2 copy-start.18
  301.6 197.2 %reduce-scatter.15.cloned.1.call-start = ((), (), s32[]{:S(2)}) async-start(), calls=%async_computation.15 | async-start | bytes 946176 | tf_op jit(solution)/shard_map/reduce_scatter | solution.py:193
  303.5 287.9 %reduce-scatter.11.cloned.1.call-start = ((), (), s32[]{:S(2)}) async-start(), calls=%async_computation.13 | async-start | bytes 6623232 | tf_op jit(solution)/shard_map/reduce_scatter | solution.py:187
  309.6 1.8 copy-start.30
  309.6 1.9 copy-start.33
  309.6 374.2 %reduce-scatter.17.cloned.1.call-start = ((), (), s32[]{:S(2)}) async-start(), calls=%async_computation.16 | async-start | bytes 6623232 | tf_op jit(solution)/shard_map/reduce_scatter | solution.py:196
  317.3 0.7 copy-start.21
  320.0 363.8 %copy-start.1 = (bf16[384,896]{1,0:T(8,128)(2,1)S(1)}, bf16[384,896]{1,0:T(8,128)(2,1)}, u32[]{:S(2)}) copy-start(bf16[384,896]{1,0:T(8,128)(2,1)} %param.8) | copy-start | bytes 2064388
  321.1 22.4 %all-to-all-start.1 = ((bf16[32,12,896]{2,1,0:T(8,128)(2,1)}), bf16[32,12,896]{2,1,0:T(8,128)(2,1)S(1)}, u32[]{:S(2)}, u32[]{:S(2)}) async-start(bf16[32,12,896]{2,1,0:T(8,128)(2,1)} %reshape.315), calls=%async_computation.1 | async-start | bytes 1835008 | tf_op jit(solution)/shard_map/all_to_all | solution.py:149
Sparse Core Ops, SparseCore 0:
  66.0 37.8 all-gather.4
  106.2 49.9 all-gather.6
  158.5 35.0 all-gather.10
  195.7 49.5 all-gather.8
  270.3 33.7 reduce-scatter.18
  306.4 34.7 reduce-scatter.20
  345.4 74.8 reduce-scatter.12
  424.4 74.3 reduce-scatter.14
  503.2 88.0 reduce-scatter.10
  595.7 88.1 reduce-scatter.16
where the time goes:
time: 700 us; the launch traced here: 691 us
  waiting for transfers between devices  437 us (62%)
  blocking collectives  75.2 us (11%)
  local copies, waits for them, and re-layouts  75.1 us (11%)
  matrix products  65.8 us (9%)
  between operations  14.9 us (2%)
  starting transfers between devices  14 us (2%)
  other arithmetic  9.05 us (1%)
    reduce_scatter x1, waiting for transfers between devices, local(): lax.psum_scatter(grad_q_part.astype(jnp.bfloat16), 'dp', scatter_dimensio...  92.6 us
    reduce_scatter x1, waiting for transfers between devices, local(): lax.psum_scatter(grad_out_part.astype(jnp.bfloat16), 'dp', scatter_dimens...  92.4 us
    reduce_scatter x1, waiting for transfers between devices, local(): lax.psum_scatter(grad_v_part.astype(jnp.bfloat16), 'dp', scatter_dimensio...  78.5 us
    reduce_scatter x1, waiting for transfers between devices, local(): lax.psum_scatter(grad_k_part.astype(jnp.bfloat16), 'dp', scatter_dimensio...  75.2 us
    all_gather x1, waiting for transfers between devices, local(): lax.all_gather(w_out, 'dp', axis=1, tiled=True)  51.8 us
    scatter x1, local copies, waits for them, and re-layouts, local(): jnp.zeros(route.shape, jnp.int32).at[route]  45.4 us
    all_gather x1, blocking collectives, local(): lax.all_gather(w_value, 'dp', axis=0, tiled=True)  27.2 us
    all_gather x1, waiting for transfers between devices, local(): c_full = lax.all_gather(inbound(c_recv), 'fs', axis=1, tiled=True)  26.1 us
  transfers between devices with their start and end apart: 12, of which 8 were waited for; matrix products, arithmetic and copies ran while one was open for 17% of the time, Pallas kernels for 0%

commit v1 on v0

v1 whole, which is shorter than its diff:
```python
import jax
import jax.numpy as jnp
from jax import lax
from jax.sharding import PartitionSpec as P

HS = 128
NZ, NX, NC = 4, 4, 2
theta_base = 1000000.0
f32 = jnp.float32
bf16 = jnp.bfloat16


def doc_layout(lengths, count_rows):
    ends = jnp.cumsum(lengths)
    starts = ends - lengths
    rows = jnp.arange(count_rows, dtype=jnp.int32)
    doc_of = jnp.sum((rows[:, None] >= ends[None, :]).astype(jnp.int32), axis=1)
    which = doc_of[:, None] == jnp.arange(lengths.shape[0], dtype=jnp.int32)[None, :]
    start_of = jnp.sum(jnp.where(which, starts[None, :], 0), axis=1)
    position = rows - start_of
    allowed = (doc_of[:, None] == doc_of[None, :]) & (rows[None, :] <= rows[:, None])
    return (position, allowed)


def angles(position, width):
    freq = theta_base ** (-(jnp.arange(width // 2, dtype=jnp.float32) * 2.0) / width)
    phase = position.astype(jnp.float32)[:, None] * freq[None, :]
    return (jnp.cos(phase), jnp.sin(phase))


def rotate(values, cosine, sine):
    half = values.shape[-1] // 2
    first = values[..., :half]
    second = values[..., half:]
    cos_b = cosine[:, None, :]
    sin_b = sine[:, None, :]
    return jnp.concatenate(
        [first * cos_b - second * sin_b, second * cos_b + first * sin_b], axis=-1
    )


def unrotate(grads, cosine, sine):
    return rotate(grads, cosine, -sine)


def attend_forward(query, keys, values, allowed, scale):
    scores = jnp.einsum("qcgd,kcd->cgqk", query, keys, preferred_element_type=f32) * scale
    scores = jnp.where(allowed[None, None], scores, -1e30)
    top = jnp.max(scores, axis=-1, keepdims=True)
    expo = jnp.exp(scores - top)
    probs = expo / jnp.sum(expo, axis=-1, keepdims=True)
    probs_low = probs.astype(bf16)
    attended = jnp.einsum("cgqk,kcd->qcgd", probs_low, values, preferred_element_type=f32)
    return (attended.astype(bf16), probs, probs_low)


def attend_backward(query, keys, values, attended, d_att, probs, probs_low, scale):
    d_probs = jnp.einsum("qcgd,kcd->cgqk", d_att, values, preferred_element_type=f32)
    delta = jnp.einsum("qcgd,qcgd->cgq", d_att, attended, preferred_element_type=f32)
    d_scores = (probs * (d_probs - delta[..., None]) * scale).astype(bf16)
    d_query = jnp.einsum("cgqk,kcd->qcgd", d_scores, keys, preferred_element_type=f32)
    d_keys = jnp.einsum("cgqk,qcgd->kcd", d_scores, query, preferred_element_type=f32)
    d_values = jnp.einsum("cgqk,qcgd->kcd", probs_low, d_att, preferred_element_type=f32)
    return (d_query, d_keys, d_values.astype(bf16))


def contract_rows(left, right):
    return lax.dot_general(left, right, (((0,), (0,)), ((), ())), preferred_element_type=f32)


def contract_cols(left, right):
    return lax.dot_general(left, right, (((1,), (1,)), ((), ())), preferred_element_type=f32)


def dp_index(z, x, c):
    return ((z % NZ) * NX + x % NX) * NC + c % NC


DP_ALL = [(z, x, c) for z in range(NZ) for x in range(NX) for c in range(NC)]
PERMS = {
    "z": lambda s: [(dp_index(z, x, c), dp_index(z + s, x, c)) for z, x, c in DP_ALL],
    "x": lambda s: [(dp_index(z, x, c), dp_index(z, x + s, c)) for z, x, c in DP_ALL],
    "core": lambda s: [(dp_index(z, x, c), dp_index(z, x, c + s)) for z, x, c in DP_ALL],
}


def shift(values, axis, step):
    if axis == "fs":
        return lax.ppermute(values, "fs", [(i, (i + step) % 4) for i in range(4)])
    return lax.ppermute(values, "dp", PERMS[axis](step))


def add(*terms):
    return sum([term.astype(f32) for term in terms]).astype(bf16)


def ring_gather(own, axis, split):
    below = shift(own, axis, 1)
    above = shift(own, axis, -1)
    far_one = shift(below[:split], axis, 1)
    far_two = shift(above[split:], axis, -1)
    return [own, above, jnp.concatenate([far_one, far_two], axis=0), below]


def ring_scatter(pieces, axis, split):
    down = shift(pieces[2][:split], axis, 1)
    up = shift(pieces[2][split:], axis, -1)
    one = jnp.concatenate([add(pieces[1][:split], down), pieces[1][split:]], axis=0)
    three = jnp.concatenate([pieces[3][:split], add(pieces[3][split:], up)], axis=0)
    return add(pieces[0], shift(one, axis, 1), shift(three, axis, -1))


def rolled(stack, start):
    return lax.dynamic_slice_in_dim(jnp.concatenate([stack, stack], axis=0), start % 4, 4, axis=0)


def local(tokens, cotangent, w_query, w_key, w_value, w_out, route, doc_lengths):
    count_dp = lax.axis_size("dp")
    my_index = lax.axis_index("dp")
    my_fs = lax.axis_index("fs")
    my_z, my_x, my_c = my_index // 8, (my_index // 2) % 4, my_index % 2
    count_rows, width = tokens.shape
    piece_rows = count_rows // count_dp
    shard = w_query.shape[0]
    scale = HS ** (-0.5)

    w_qkv = lax.all_gather(
        jnp.concatenate([w_query, w_key, w_value], axis=1), "dp", axis=0, tiled=True
    )
    w_out_t = lax.all_gather(w_out.T, "dp", axis=0, tiled=True)

    line_ids = jnp.arange(count_rows, dtype=jnp.int32)
    own_route = lax.dynamic_slice_in_dim(route, my_index * count_rows, count_rows)
    send_rank = jnp.sum((own_route[None, :] < own_route[:, None]).astype(jnp.int32), axis=1)
    send_table = (send_rank[None, :] == line_ids[:, None]).astype(bf16)

    planned = my_index * count_rows + line_ids
    home_block = jnp.arange(route.shape[0], dtype=jnp.int32) // count_rows
    source = jnp.sum(jnp.where(route[None, :] == planned[:, None], home_block[None, :], 0), axis=1)
    earlier = (source[None, :] == source[:, None]) & (line_ids[None, :] < line_ids[:, None])
    buffer_row = source * piece_rows + jnp.sum(earlier.astype(jnp.int32), axis=1)
    recv_table = (buffer_row[:, None] == line_ids[None, :]).astype(bf16)

    def outbound(values):
        moved = jnp.dot(send_table, values, preferred_element_type=f32).astype(bf16)
        return moved.reshape(count_dp, piece_rows, values.shape[1])

    def inbound(values):
        flat_in = values.reshape(count_rows, values.shape[2])
        return jnp.dot(recv_table, flat_in, preferred_element_type=f32).astype(bf16)

    def swap(values):
        return lax.all_to_all(values, "dp", split_axis=0, concat_axis=0, tiled=True)

    def whole(own):
        pieces = jnp.stack(ring_gather(own, "fs", count_rows // 2), axis=0)
        return rolled(pieces, 4 - my_fs)

    def flat_of(blocks):
        return blocks.transpose(1, 0, 2).reshape(count_rows, 4 * width)

    x_blocks = whole(inbound(swap(outbound(tokens))))
    x_full = flat_of(x_blocks)
    c_blocks = whole(inbound(swap(outbound(cotangent))))
    c_full = flat_of(c_blocks)

    heads_here = w_query.shape[1] // HS
    kv_here = w_key.shape[1] // HS
    groups = heads_here // kv_here
    q_width, kv_width = heads_here * HS, kv_here * HS
    position, allowed = doc_layout(doc_lengths[0], count_rows)
    cosine, sine = angles(position, HS)
    qkv = jnp.dot(x_full, w_qkv, preferred_element_type=f32)
    query = (
        rotate(qkv[:, :q_width].reshape(count_rows, heads_here, HS), cosine, sine)
        .astype(bf16)
        .reshape(count_rows, kv_here, groups, HS)
    )
    keys = rotate(
        qkv[:, q_width : q_width + kv_width].reshape(count_rows, kv_here, HS), cosine, sine
    ).astype(bf16)
    values = qkv[:, q_width + kv_width :].astype(bf16).reshape(count_rows, kv_here, HS)
    attended, probs, probs_low = attend_forward(query, keys, values, allowed, scale)
    flat = attended.reshape(count_rows, heads_here * HS)

    head_part = contract_cols(flat, w_out_t).astype(bf16)
    head_blocks = rolled(head_part.reshape(count_rows, 4, width).transpose(1, 0, 2), my_fs)
    out_planned = ring_scatter(
        [head_blocks[r] for r in range(4)], "fs", count_rows // 2
    )
    going_home = contract_rows(recv_table, out_planned).astype(bf16)
    returned = swap(going_home.reshape(count_dp, piece_rows, width)).reshape(count_rows, width)
    out_home = contract_rows(send_table, returned).astype(bf16)

    d_att = (
        jnp.dot(c_full, w_out_t, preferred_element_type=f32)
        .astype(bf16)
        .reshape(count_rows, kv_here, groups, HS)
    )
    grad_out_part = contract_rows(c_full, flat).astype(bf16)
    wo_sum = lax.psum_scatter(grad_out_part, "dp", scatter_dimension=0, tiled=True).T

    d_query, d_keys, d_values = attend_backward(
        query, keys, values, attended, d_att, probs, probs_low, scale
    )
    dq_flat = unrotate(d_query.reshape(count_rows, heads_here, HS), cosine, sine).astype(bf16)
    dk_flat = unrotate(d_keys, cosine, sine).astype(bf16)
    d_qkv = jnp.concatenate(
        [
            dq_flat.reshape(count_rows, q_width),
            dk_flat.reshape(count_rows, kv_width),
            d_values.reshape(count_rows, kv_width),
        ],
        axis=1,
    )

    order = jnp.arange(width, dtype=jnp.int32)
    rel_c, rel_x, lane = order // (4 * shard), (order // shard) % 4, order % shard
    feature = ((my_x + rel_x) % 4 * 2 + (my_c + rel_c) % 2) * shard + lane
    pick = (feature[:, None] == order[None, :]).astype(bf16)
    x_by_z = rolled(x_blocks, my_z)
    x_rel = [contract_cols(pick, x_by_z[r]).astype(bf16) for r in range(4)]
    half = 4 * shard
    x_own = jnp.concatenate([block[:half] for block in x_rel], axis=0)
    x_other = jnp.concatenate([block[half:] for block in x_rel], axis=0)

    def x_major(rows):
        return rows.reshape(4, 4, shard, count_rows).transpose(1, 0, 2, 3).reshape(-1, count_rows)

    cut = 5 * HS

    def reduced(own_rows, other_rows, cols, first, second):
        there = jnp.dot(other_rows, cols, preferred_element_type=f32).astype(bf16)
        came = shift(there, "core", 1)
        here = jnp.dot(own_rows, cols, preferred_element_type=f32).astype(bf16)
        both = add(here, came).reshape(4, 4, shard, cols.shape[1])
        line = ring_scatter([both[r] for r in range(4)], first, 2)
        return ring_scatter([line[r] for r in range(4)], second, 64)

    part_a = reduced(x_own, x_other, d_qkv[:, :cut], "z", "x")
    part_b = reduced(x_major(x_own), x_major(x_other), d_qkv[:, cut:], "x", "z")
    grad_q = jnp.concatenate([part_a, part_b[:, : q_width - cut]], axis=1)
    grad_k = part_b[:, q_width - cut : q_width - cut + kv_width]
    grad_v = part_b[:, q_width - cut + kv_width :]

    grad_rows = contract_cols(d_qkv, w_qkv).astype(bf16)
    grad_blocks = rolled(grad_rows.reshape(count_rows, 4, width).transpose(1, 0, 2), my_fs)
    grad_in = ring_scatter([grad_blocks[r] for r in range(4)], "fs", count_rows // 2)

    return (out_home, grad_in, grad_q, grad_k, grad_v, wo_sum)


def solution(mesh):
    in_specs = (
        P("dp", "fs"),
        P("dp", "fs"),
        P("dp", "fs"),
        P("dp", "fs"),
        P("dp", "fs"),
        P("fs", "dp"),
        P(),
        P("dp", None),
    )
    out_specs = (
        P("dp", "fs"),
        P("dp", "fs"),
        P("dp", "fs"),
        P("dp", "fs"),
        P("dp", "fs"),
        P("fs", "dp"),
    )
    return jax.shard_map(local, mesh=mesh, in_specs=in_specs, out_specs=out_specs, check_vma=False)
```

time: 700 us -> 334 us (0.48)
  waiting for transfers between devices: 437 us -> 110 us
  blocking collectives: 75.2 us -> 0 us
  starting transfers between devices: 14 us -> 66 us
  local copies, waits for them, and re-layouts: 75.1 us -> 34.9 us
  other arithmetic: 9.05 us -> 26.8 us
  matrix products: 65.8 us -> 76.7 us
    reduce_scatter x4 -> x1, waiting for transfers between devices: 339 us -> 0.01 us  [local(): lax.psum_scatter(grad_out_part, 'dp', scatter_dimension=0, tiled=True)]
    all_gather x4 -> x2, waiting for transfers between devices: 81.3 us -> 0.01 us  [the longest x1 0.01 us: local(): w_out_t = lax.all_gather(w_out.T, 'dp', axis=0, tiled=True)]
    ppermute x0 -> x34, waiting for transfers between devices: none -> 69.9 us  [the longest x18 35.5 us: shift(): return lax.ppermute(values, 'dp', PERMS[axis](step))]
    all_gather x2 -> x0, blocking collectives: 52.1 us -> none  [the longest x1 27.2 us: local(): lax.all_gather(w_value, 'dp', axis=0, tiled=True)]
    ppermute x0 -> x34, starting transfers between devices: none -> 48.6 us  [the longest x16 25.8 us: shift(): return lax.ppermute(values, 'fs', [(i, (i + step) % 4) for i in range(4)])]
    scatter x1 -> x0, local copies, waits for them, and re-layouts: 45.4 us -> none  [local(): jnp.zeros(route.shape, jnp.int32).at[route]]
    all_to_all x2 -> x3, waiting for transfers between devices: 0.01 us -> 39.3 us  [swap(): return lax.all_to_all(values, 'dp', split_axis=0, concat_axis=0, tiled=True)]
    all_to_all x1 -> x0, blocking collectives: 23.1 us -> none  [local(): lax.all_to_all(outbound(cotangent), 'dp', split_axis=0, concat_axis=0, ti...]
  transfers between devices with their start and end apart: 12 -> 40, of which waited for: 8 -> 21; matrix products, arithmetic and copies ran while one was open for 17% -> 26% of each run, Pallas kernels for 0% -> 0%
where the time goes in v1:
time: 334 us; the launch traced here: 329 us
  waiting for transfers between devices  110 us (33%)
  matrix products  76.7 us (23%)
  starting transfers between devices  66 us (20%)
  local copies, waits for them, and re-layouts  34.9 us (10%)
  other arithmetic  26.8 us (8%)
  between operations  15.2 us (5%)
    all_to_all x3, waiting for transfers between devices, swap(): return lax.all_to_all(values, 'dp', split_axis=0, concat_axis=0, tiled=True)  39.3 us
    ppermute x18, waiting for transfers between devices, shift(): return lax.ppermute(values, 'dp', PERMS[axis](step))  35.5 us
    ppermute x16, waiting for transfers between devices, shift(): return lax.ppermute(values, 'fs', [(i, (i + step) % 4) for i in range(4)])  34.4 us
    ppermute x16, starting transfers between devices, shift(): return lax.ppermute(values, 'fs', [(i, (i + step) % 4) for i in range(4)])  25.8 us
    ppermute x18, starting transfers between devices, shift(): return lax.ppermute(values, 'dp', PERMS[axis](step))  22.8 us
    dot_general x1, matrix products, local(): qkv = jnp.dot(x_full, w_qkv, preferred_element_type=f32)  18.1 us
    dot_general x6, matrix products, contract_cols(): lax.dot_general(left, right, (((1,), (1,)), ((), ())), preferred_element_...  17.6 us
    all_to_all x3, starting transfers between devices, swap(): return lax.all_to_all(values, 'dp', split_axis=0, concat_axis=0, tiled=True)  17.3 us
  transfers between devices with their start and end apart: 40, of which 21 were waited for; matrix products, arithmetic and copies ran while one was open for 26% of the time, Pallas kernels for 0%

profile of v1, /device:TPU:0, one launch (start us, length us, event | category | flops | bytes accessed | tf_op | source)
XLA Modules:
  0.0 329.5 jit_solution(7297915245758064963)
XLA Ops:
  8.0 1.7 pad_maximum_fusion.13
  12.4 8.4 %all-to-all-start.2 = ((bf16[32,12,896]{2,1,0:T(8,128)(2,1)}), bf16[32,12,896]{2,1,0:T(8,128)(2,1)S(1)}, u32[]{:S(2)}, u32[]{:S(2)}) async-start(bf16[32,12,896]{2,1,0:T(8,128)(2,1)} %reshape.565), calls=%async_computation.2 | async-start | bytes 1835008 | tf_op jit(solution)/shard_map/all_to_all | solution.py:153
  22.9 2.3 select_reduce_fusion
  25.2 14.0 %all-to-all-done.2 = bf16[32,12,896]{2,1,0:T(8,128)(2,1)S(1)} async-done(((bf16[32,12,896]{2,1,0:T(8,128)(2,1)}), bf16[32,12,896]{2,1,0:T(8,128)(2,1)S(1)}, u32[]{:S(2)}, u32[]{:S(2)}) %all-to-all-start.2) | async-done | bytes 688160 | tf_op jit(solution)/shard_map/all_to_all | solution.py:153
  39.3 3.9 %all-to-all-start = ((bf16[32,12,896]{2,1,0:T(8,128)(2,1)}), bf16[32,12,896]{2,1,0:T(8,128)(2,1)S(1)}, u32[]{:S(2)}, u32[]{:S(2)}) async-start(bf16[32,12,896]{2,1,0:T(8,128)(2,1)} %reshape.553), calls=%async_computation | async-start | bytes 1835008 | tf_op jit(solution)/shard_map/all_to_all | solution.py:153
  43.7 1.4 bitcast_dynamic-update-slice_fusion.4
  45.2 3.0 collective-permute-start.8
  48.2 15.5 %all-to-all-done = bf16[32,12,896]{2,1,0:T(8,128)(2,1)S(1)} async-done(((bf16[32,12,896]{2,1,0:T(8,128)(2,1)}), bf16[32,12,896]{2,1,0:T(8,128)(2,1)S(1)}, u32[]{:S(2)}, u32[]{:S(2)}) %all-to-all-start) | async-done | bytes 688160 | tf_op jit(solution)/shard_map/all_to_all | solution.py:153
  64.6 1.8 bitcast_dynamic-update-slice_fusion.10
  66.5 3.4 %collective-permute-start = (bf16[384,896]{1,0:T(8,128)(2,1)S(1)}, bf16[384,896]{1,0:T(8,128)(2,1)S(1)}, u32[]{:S(2)}, u32[]{:S(2)}) collective-permute-start(bf16[384,896]{1,0:T(8,128)(2,1)S(1)} %get-tuple-element.62), channel_id=1, source_target_pairs={{0,3},{1,0},{2,1},{3,2},{4,7},{5,4},{6,5},{7,6},{8,11},{9,8},{10,9... | collective-permute-start | bytes 2064392 | tf_op jit(solution)/shard_map/ppermute | solution.py:89
  70.7 1.6 fusion.118
  72.3 3.3 %collective-permute-start.11 = (bf16[192,896]{1,0:T(8,128)(2,1)S(1)}, bf16[192,896]{1,0:T(8,128)(2,1)S(1)}, u32[]{:S(2)}, u32[]{:S(2)}) collective-permute-start(bf16[192,896]{1,0:T(8,128)(2,1)S(1)} %slice.484), channel_id=1, source_target_pairs={{0,3},{1,0},{2,1},{3,2},{4,7},{5,4},{6,5},{7,6},{8,11},{9,8},{10,9... | collective-permute-start | bytes 1032200 | tf_op jit(solution)/shard_map/ppermute | solution.py:89
  75.7 10.0 %collective-permute-done = bf16[384,896]{1,0:T(8,128)(2,1)S(1)} collective-permute-done((bf16[384,896]{1,0:T(8,128)(2,1)S(1)}, bf16[384,896]{1,0:T(8,128)(2,1)S(1)}, u32[]{:S(2)}, u32[]{:S(2)}) %collective-permute-start) | collective-permute-done | bytes 688160 | tf_op jit(solution)/shard_map/ppermute | solution.py:89
  85.8 3.8 %collective-permute-start.3 = (bf16[192,896]{1,0:T(8,128)(2,1)S(1)}, bf16[192,896]{1,0:T(8,128)(2,1)S(1)}, u32[]{:S(2)}, u32[]{:S(2)}) collective-permute-start(bf16[192,896]{1,0:T(8,128)(2,1)S(1)} %slice.468), channel_id=1, source_target_pairs={{0,3},{1,0},{2,1},{3,2},{4,7},{5,4},{6,5},{7,6},{8,11},{9,8},{10,9... | collective-permute-start | bytes 1032200 | tf_op jit(solution)/shard_map/ppermute | solution.py:89
  89.9 3.3 collective-permute-done.11
  93.2 3.7 %collective-permute-done.10 = bf16[192,896]{1,0:T(8,128)(2,1)S(1)} collective-permute-done((bf16[192,896]{1,0:T(8,128)(2,1)S(1)}, bf16[192,896]{1,0:T(8,128)(2,1)S(1)}, u32[]{:S(2)}, u32[]{:S(2)}) %collective-permute-start.10) | collective-permute-done | bytes 344096 | tf_op jit(solution)/shard_map/ppermute | solution.py:89
  97.3 1.5 collective-permute-done.3
  98.8 3.4 %collective-permute-done.2 = bf16[192,896]{1,0:T(8,128)(2,1)S(1)} collective-permute-done((bf16[192,896]{1,0:T(8,128)(2,1)S(1)}, bf16[192,896]{1,0:T(8,128)(2,1)S(1)}, u32[]{:S(2)}, u32[]{:S(2)}) %collective-permute-start.2) | collective-permute-done | bytes 344096 | tf_op jit(solution)/shard_map/ppermute | solution.py:89
  103.0 2.1 dynamic-slice_bitcast_fusion
  105.0 4.8 %copy.65 = bf16[384,4,896]{0,2,1:T(8,128)(2,1)} copy(bf16[384,4,896]{2,0,1:T(8,128)(2,1)} %get-tuple-element.69) | data formatting | bytes 5505024 | tf_op jit(solution)/shard_map/transpose | solution.py:160
  109.9 2.8 copy.58
  121.4 7.0 %convolution_convert_fusion.7 = bf16[384,896]{1,0:T(8,128)(2,1)S(1)} fusion(bf16[384,3584]{0,1:T(8,128)(2,1)} %bitcast.337, bf16[3584,896]{1,0:T(8,128)(2,1)} %all-gather.5.cloned.1.call-done), kind=kOutput, calls=%fused_computation.64 | convolution fusion | flops 2466594816 | bytes 9863168 | tf_op jit(solution)/shard_map/dot_general | solution.py:196
  129.6 18.1 %fusion.159 = f32[384,1152]{1,0:T(8,128)S(1)} fusion(bf16[384,3584]{0,1:T(8,128)(2,1)S(1)} %bitcast.331, bf16[3584,1152]{1,0:T(8,128)(2,1)} %all-gather.3.cloned.1.call-done), kind=kOutput, calls=%fused_computation.301 | convolution fusion | flops 3170893824 | bytes 12779520 | tf_op jit(solution)/shard_map/dot_general | solution.py:173
  151.1 1.9 fusion.115
  153.0 1.4 subtract_convert_fusion.1
  156.7 2.4 fusion.33
  159.1 1.4 fusion.52
  160.4 2.7 fusion.2
  165.7 5.6 %convolution_convert_fusion = bf16[3584,896]{1,0:T(8,128)(2,1)} fusion(bf16[384,3584]{0,1:T(8,128)(2,1)S(1)} %bitcast.338, bf16[384,896]{0,1:T(8,128)(2,1)S(1)} %bitcast.368), kind=kOutput, calls=%fused_computation.1 | convolution fusion | flops 2469462016 | bytes 9863168 | tf_op jit(solution)/shard_map/dot_general | solution.py:68
  171.3 5.9 %convolution_convert_fusion.2 = bf16[384,3584]{1,0:T(8,128)(2,1)S(1)} fusion(bf16[384,896]{0,1:T(8,128)(2,1)S(1)} %bitcast.369, bf16[3584,896]{1,0:T(8,128)(2,1)} %all-gather.5.cloned.1.call-done), kind=kOutput, calls=%fused_computation.3 | convolution fusion | flops 2467627008 | bytes 9863168 | tf_op jit(solution)/shard_map/dot_general | solution.py:72
  178.6 1.5 copy-done.3
  181.2 3.6 %collective-permute-start.6 = (bf16[192,896]{1,0:T(8,128)(2,1)}, bf16[192,896]{1,0:T(8,128)(2,1)}, u32[]{:S(2)}, u32[]{:S(2)}) collective-permute-start(bf16[192,896]{1,0:T(8,128)(2,1)} %get-tuple-element.19), channel_id=1, source_target_pairs={{0,3},{1,0},{2,1},{3,2},{4,7},{5,4},{6,5},{7,6},{8,11},{9,8},{10,9... | collective-permute-start | bytes 1032200 | tf_op jit(solution)/shard_map/ppermute | solution.py:89
  187.2 7.3 %convolution_convert_fusion.1 = bf16[384,3584]{1,0:T(8,128)(2,1)S(1)} fusion(bf16[3584,1152]{1,0:T(8,128)(2,1)} %all-gather.3.cloned.1.call-done, bf16[384,128]{0,1:T(8,128)(2,1)S(1)} %fusion.52, bf16[384,64]{0,1:T(8,128)(2,1)S(1)} %copy.77, bf16[384,64]{0,1:T(8,128)(2,1)S(1)} %copy.76, bf16[384,896]{0,1:T(8,128)(2,1)S(1)} %bitcast.353), kind=kOutput, calls=%fused_computation.2 | convolution fusion | flops 3175809024 | bytes 11894784 | tf_op jit(solution)/shard_map/dot_general | solution.py:72
  196.0 2.5 convolution_convert_fusion.5
  200.0 3.2 collective-permute-start.14
  204.7 2.1 collective-permute-start.5
  206.8 2.9 convolution_convert_fusion.3
  209.7 2.3 collective-permute-done.12
  213.3 3.1 collective-permute-start.15
  217.3 9.1 %collective-permute-done.7 = bf16[384,896]{1,0:T(8,128)(2,1)S(1)} collective-permute-done((bf16[384,896]{1,0:T(8,128)(2,1)S(1)}, bf16[384,896]{1,0:T(8,128)(2,1)S(1)}, u32[]{:S(2)}, u32[]{:S(2)}) %collective-permute-start.7) | collective-permute-done | bytes 688160 | tf_op jit(solution)/shard_map/ppermute | solution.py:89
  226.4 1.5 convolution_convert_fusion.11
  227.9 2.1 reshape.563
  229.9 5.0 %all-to-all-start.1 = ((bf16[32,12,896]{2,1,0:T(8,128)(2,1)}), bf16[32,12,896]{2,1,0:T(8,128)(2,1)}, u32[]{:S(2)}, u32[]{:S(2)}) async-start(bf16[32,12,896]{2,1,0:T(8,128)(2,1)} %reshape.563), calls=%async_computation.1 | async-start | bytes 1835008 | tf_op jit(solution)/shard_map/all_to_all | solution.py:153
  235.0 3.1 add_convert_fusion.1
  240.6 3.0 collective-permute-start.28
  244.6 2.4 fusion.30
  247.1 9.8 %all-to-all-done.1 = bf16[32,12,896]{2,1,0:T(8,128)(2,1)} async-done(((bf16[32,12,896]{2,1,0:T(8,128)(2,1)}), bf16[32,12,896]{2,1,0:T(8,128)(2,1)}, u32[]{:S(2)}, u32[]{:S(2)}) %all-to-all-start.1) | async-done | bytes 688160 | tf_op jit(solution)/shard_map/all_to_all | solution.py:153
  256.9 1.3 reshape.564
  259.4 3.4 %collective-permute-done.28 = bf16[2,112,512]{2,1,0:T(8,128)(2,1)} collective-permute-done((bf16[2,112,512]{2,1,0:T(8,128)(2,1)}, bf16[2,112,512]{2,1,0:T(8,128)(2,1)}, u32[]{:S(2)}, u32[]{:S(2)}) %collective-permute-start.28) | collective-permute-done | bytes 229408 | tf_op jit(solution)/shard_map/ppermute | solution.py:90
  265.6 3.5 %collective-permute-done.26 = bf16[2,112,512]{2,1,0:T(8,128)(2,1)S(1)} collective-permute-done((bf16[2,112,512]{2,1,0:T(8,128)(2,1)}, bf16[2,112,512]{2,1,0:T(8,128)(2,1)S(1)}, u32[]{:S(2)}, u32[]{:S(2)}) %collective-permute-start.26) | collective-permute-done | bytes 229408 | tf_op jit(solution)/shard_map/ppermute | solution.py:90
  269.8 3.1 add_convert_fusion
  273.1 2.5 collective-permute-start.19
  276.1 5.9 %collective-permute-done.27 = bf16[4,112,512]{2,1,0:T(8,128)(2,1)S(1)} collective-permute-done((bf16[4,112,512]{2,1,0:T(8,128)(2,1)S(1)}, bf16[4,112,512]{2,1,0:T(8,128)(2,1)S(1)}, u32[]{:S(2)}, u32[]{:S(2)}) %collective-permute-start.27) | collective-permute-done | bytes 458784 | tf_op jit(solution)/shard_map/ppermute | solution.py:90
  282.2 4.6 %collective-permute-start.32 = (bf16[48,512]{1,0:T(8,128)(2,1)S(1)}, bf16[48,512]{1,0:T(8,128)(2,1)S(1)}, u32[]{:S(2)}, u32[]{:S(2)}) collective-permute-start(bf16[48,512]{1,0:T(8,128)(2,1)S(1)} %get-tuple-element.51), channel_id=1, source_target_pairs={{0,96},{4,100},{8,104},{12,108},{16,112},{20,116},{24,120},{28,124... | collective-permute-start | bytes 147464 | tf_op jit(solution)/shard_map/ppermute | solution.py:90
  286.9 1.7 collective-permute-done.32
  288.6 3.6 %collective-permute-start.33 = (bf16[112,512]{1,0:T(8,128)(2,1)S(1)}, bf16[112,512]{1,0:T(8,128)(2,1)S(1)}, u32[]{:S(2)}, u32[]{:S(2)}) collective-permute-start(bf16[112,512]{1,0:T(8,128)(2,1)S(1)} %pad_maximum_fusion.18), channel_id=1, source_target_pairs={{0,96},{4,100},{8,104},{12,108},{16,112},{20,116},{24,120},{28,124... | collective-permute-start | bytes 344072 | tf_op jit(solution)/shard_map/ppermute | solution.py:90
  292.6 2.1 collective-permute-start.18
  294.8 1.4 convolution_convert_fusion.10
  296.3 12.1 %collective-permute-done.31 = bf16[112,512]{1,0:T(8,128)(2,1)S(1)} collective-permute-done((bf16[112,512]{1,0:T(8,128)(2,1)S(1)}, bf16[112,512]{1,0:T(8,128)(2,1)S(1)}, u32[]{:S(2)}, u32[]{:S(2)}) %collective-permute-start.31) | collective-permute-done | bytes 114720 | tf_op jit(solution)/shard_map/ppermute | solution.py:90
  309.1 1.8 collective-permute-start.21
  310.9 2.4 collective-permute-done.23
  313.3 1.8 collective-permute-start.24
  316.3 2.2 collective-permute-done.24
  318.5 3.5 %collective-permute-done.22 = bf16[112,640]{1,0:T(8,128)(2,1)S(1)} collective-permute-done((bf16[112,640]{1,0:T(8,128)(2,1)S(1)}, bf16[112,640]{1,0:T(8,128)(2,1)S(1)}, u32[]{:S(2)}, u32[]{:S(2)}) %collective-permute-start.22) | collective-permute-done | bytes 143392 | tf_op jit(solution)/shard_map/ppermute | solution.py:90
  (242 shorter events, 50.8 us)
Async XLA Ops:
  7.2 114.3 %all-gather.5.cloned.1.call-start = ((), (), s32[]{:S(2)}) async-start(), calls=%async_computation.5 | async-start | bytes 6623232 | tf_op jit(solution)/shard_map/all_gather | solution.py:130
  7.9 12.9 %copy-start.33 = (bf16[384,896]{1,0:T(8,128)(2,1)S(1)}, bf16[384,896]{1,0:T(8,128)(2,1)}, u32[]{:S(2)}) copy-start(bf16[384,896]{1,0:T(8,128)(2,1)} %param.8) | copy-start | bytes 2064388
  7.9 121.6 %all-gather.3.cloned.1.call-start = ((), (), s32[]{:S(2)}) async-start(), calls=%async_computation.4 | async-start | bytes 8515584 | tf_op jit(solution)/shard_map/all_gather | solution.py:127
  12.4 10.1 %copy-start.40 = (s32[1,2]{1,0:T(1,128)S(1)}, s32[1,2]{1,0:T(1,128)}, u32[]{:S(2)}) copy-start(s32[1,2]{1,0:T(1,128)} %param.15) | copy-start | bytes 28
  12.4 10.5 %copy-start.39 = (s32[12288]{0:T(1024)S(1)}, s32[12288]{0:T(1024)}, u32[]{:S(2)}) copy-start(s32[12288]{0:T(1024)} %param.14) | copy-start | bytes 147460
  12.4 26.9 %all-to-all-start.2 = ((bf16[32,12,896]{2,1,0:T(8,128)(2,1)}), bf16[32,12,896]{2,1,0:T(8,128)(2,1)S(1)}, u32[]{:S(2)}, u32[]{:S(2)}) async-start(bf16[32,12,896]{2,1,0:T(8,128)(2,1)} %reshape.565), calls=%async_computation.2 | async-start | bytes 1835008 | tf_op jit(solution)/shard_map/all_to_all | solution.py:153
  39.3 24.4 %all-to-all-start = ((bf16[32,12,896]{2,1,0:T(8,128)(2,1)}), bf16[32,12,896]{2,1,0:T(8,128)(2,1)S(1)}, u32[]{:S(2)}, u32[]{:S(2)}) async-start(bf16[32,12,896]{2,1,0:T(8,128)(2,1)} %reshape.553), calls=%async_computation | async-start | bytes 1835008 | tf_op jit(solution)/shard_map/all_to_all | solution.py:153
  43.2 279.6 %reduce-scatter.2.cloned.1.call-start = ((), (), s32[]{:S(2)}) async-start(), calls=%async_computation.6 | async-start | bytes 6623232 | tf_op jit(solution)/shard_map/reduce_scatter | solution.py:201
  45.2 27.1 %collective-permute-start.8 = (bf16[384,896]{1,0:T(8,128)(2,1)S(1)}, bf16[384,896]{1,0:T(8,128)(2,1)S(1)}, u32[]{:S(2)}, u32[]{:S(2)}) collective-permute-start(bf16[384,896]{1,0:T(8,128)(2,1)S(1)} %get-tuple-element.66), channel_id=1, source_target_pairs={{0,3},{1,0},{2,1},{3,2},{4,7},{5,4},{6,5},{7,6},{8,11},{9,8},{10,9... | collective-permute-start | bytes 2064392 | tf_op jit(solution)/shard_map/ppermute | solution.py:89
  48.2 27.5 %collective-permute-start.9 = (bf16[384,896]{1,0:T(8,128)(2,1)S(1)}, bf16[384,896]{1,0:T(8,128)(2,1)S(1)}, u32[]{:S(2)}, u32[]{:S(2)}) collective-permute-start(bf16[384,896]{1,0:T(8,128)(2,1)S(1)} %get-tuple-element.66), channel_id=1, source_target_pairs={{0,1},{1,2},{2,3},{3,0},{4,5},{5,6},{6,7},{7,4},{8,9},{9,10},{10,1... | collective-permute-start | bytes 2064392 | tf_op jit(solution)/shard_map/ppermute | solution.py:89
  64.6 25.1 %copy-start.9 = (bf16[8,384,896]{2,1,0:T(8,128)(2,1)S(1)}, bf16[8,384,896]{2,1,0:T(8,128)(2,1)}, u32[]{:S(2)}) copy-start(bf16[8,384,896]{2,1,0:T(8,128)(2,1)} %get-tuple-element.65) | copy-start | bytes 16515076
  66.5 19.3 %collective-permute-start = (bf16[384,896]{1,0:T(8,128)(2,1)S(1)}, bf16[384,896]{1,0:T(8,128)(2,1)S(1)}, u32[]{:S(2)}, u32[]{:S(2)}) collective-permute-start(bf16[384,896]{1,0:T(8,128)(2,1)S(1)} %get-tuple-element.62), channel_id=1, source_target_pairs={{0,3},{1,0},{2,1},{3,2},{4,7},{5,4},{6,5},{7,6},{8,11},{9,8},{10,9... | collective-permute-start | bytes 2064392 | tf_op jit(solution)/shard_map/ppermute | solution.py:89
  69.9 19.7 %collective-permute-start.1 = (bf16[384,896]{1,0:T(8,128)(2,1)S(1)}, bf16[384,896]{1,0:T(8,128)(2,1)S(1)}, u32[]{:S(2)}, u32[]{:S(2)}) collective-permute-start(bf16[384,896]{1,0:T(8,128)(2,1)S(1)} %get-tuple-element.62), channel_id=1, source_target_pairs={{0,1},{1,2},{2,3},{3,0},{4,5},{5,6},{6,7},{7,4},{8,9},{9,10},{10,1... | collective-permute-start | bytes 2064392 | tf_op jit(solution)/shard_map/ppermute | solution.py:89
  72.3 20.8 %collective-permute-start.11 = (bf16[192,896]{1,0:T(8,128)(2,1)S(1)}, bf16[192,896]{1,0:T(8,128)(2,1)S(1)}, u32[]{:S(2)}, u32[]{:S(2)}) collective-permute-start(bf16[192,896]{1,0:T(8,128)(2,1)S(1)} %slice.484), channel_id=1, source_target_pairs={{0,3},{1,0},{2,1},{3,2},{4,7},{5,4},{6,5},{7,6},{8,11},{9,8},{10,9... | collective-permute-start | bytes 1032200 | tf_op jit(solution)/shard_map/ppermute | solution.py:89
  75.7 21.2 %collective-permute-start.10 = (bf16[192,896]{1,0:T(8,128)(2,1)S(1)}, bf16[192,896]{1,0:T(8,128)(2,1)S(1)}, u32[]{:S(2)}, u32[]{:S(2)}) collective-permute-start(bf16[192,896]{1,0:T(8,128)(2,1)S(1)} %slice.483), channel_id=1, source_target_pairs={{0,1},{1,2},{2,3},{3,0},{4,5},{5,6},{6,7},{7,4},{8,9},{9,10},{10,1... | collective-permute-start | bytes 1032200 | tf_op jit(solution)/shard_map/ppermute | solution.py:89
  85.8 13.0 %collective-permute-start.3 = (bf16[192,896]{1,0:T(8,128)(2,1)S(1)}, bf16[192,896]{1,0:T(8,128)(2,1)S(1)}, u32[]{:S(2)}, u32[]{:S(2)}) collective-permute-start(bf16[192,896]{1,0:T(8,128)(2,1)S(1)} %slice.468), channel_id=1, source_target_pairs={{0,3},{1,0},{2,1},{3,2},{4,7},{5,4},{6,5},{7,6},{8,11},{9,8},{10,9... | collective-permute-start | bytes 1032200 | tf_op jit(solution)/shard_map/ppermute | solution.py:89
  89.6 12.7 %collective-permute-start.2 = (bf16[192,896]{1,0:T(8,128)(2,1)S(1)}, bf16[192,896]{1,0:T(8,128)(2,1)S(1)}, u32[]{:S(2)}, u32[]{:S(2)}) collective-permute-start(bf16[192,896]{1,0:T(8,128)(2,1)S(1)} %slice.467), channel_id=1, source_target_pairs={{0,1},{1,2},{2,3},{3,0},{4,5},{5,6},{6,7},{7,4},{8,9},{9,10},{10,1... | collective-permute-start | bytes 1032200 | tf_op jit(solution)/shard_map/ppermute | solution.py:89
  121.4 8.1 %copy-start.2 = (bf16[384,4,896]{0,2,1:T(8,128)(2,1)S(1)}, bf16[384,4,896]{0,2,1:T(8,128)(2,1)}, u32[]{:S(2)}) copy-start(bf16[384,4,896]{0,2,1:T(8,128)(2,1)} %copy.58) | copy-start | bytes 8257540
  160.4 34.4 %copy-start.41 = (bf16[384,128]{0,1:T(8,128)(2,1)}, bf16[384,128]{0,1:T(8,128)(2,1)S(1)}, u32[]{:S(2)}) copy-start(bf16[384,128]{0,1:T(8,128)(2,1)S(1)} %fusion.52) | copy-start | bytes 294916
  180.1 5.8 %copy-start.8 = (f32[384,64]{1,0:T(8,128)S(1)}, f32[384,64]{1,0:T(8,128)}, u32[]{:S(2)}) copy-start(f32[384,64]{1,0:T(8,128)} %get-tuple-element.60) | copy-start | bytes 294916
  180.1 5.8 %copy-start.32 = (f32[384,64]{1,0:T(8,128)S(1)}, f32[384,64]{1,0:T(8,128)}, u32[]{:S(2)}) copy-start(f32[384,64]{1,0:T(8,128)} %get-tuple-element.58) | copy-start | bytes 294916
  181.2 22.0 %collective-permute-start.4 = (bf16[192,896]{1,0:T(8,128)(2,1)}, bf16[192,896]{1,0:T(8,128)(2,1)}, u32[]{:S(2)}, u32[]{:S(2)}) collective-permute-start(bf16[192,896]{1,0:T(8,128)(2,1)} %get-tuple-element.16), channel_id=1, source_target_pairs={{0,1},{1,2},{2,3},{3,0},{4,5},{5,6},{6,7},{7,4},{8,9},{9,10},{10,1... | collective-permute-start | bytes 1032200 | tf_op jit(solution)/shard_map/ppermute | solution.py:89
  181.2 22.0 %collective-permute-start.6 = (bf16[192,896]{1,0:T(8,128)(2,1)}, bf16[192,896]{1,0:T(8,128)(2,1)}, u32[]{:S(2)}, u32[]{:S(2)}) collective-permute-start(bf16[192,896]{1,0:T(8,128)(2,1)} %get-tuple-element.19), channel_id=1, source_target_pairs={{0,3},{1,0},{2,1},{3,2},{4,7},{5,4},{6,5},{7,6},{8,11},{9,8},{10,9... | collective-permute-start | bytes 1032200 | tf_op jit(solution)/shard_map/ppermute | solution.py:89
  187.2 7.6 %copy-start.34 = (bf16[384,7,128]{0,2,1:T(8,128)(2,1)}, bf16[384,7,128]{0,2,1:T(8,128)(2,1)S(1)}, u32[]{:S(2)}) copy-start(bf16[384,7,128]{0,2,1:T(8,128)(2,1)S(1)} %copy.71) | copy-start | bytes 2064388
  199.6 35.3 %collective-permute-start.25 = (bf16[1792,512]{1,0:T(8,128)(2,1)}, bf16[1792,512]{1,0:T(8,128)(2,1)}, u32[]{:S(2)}, u32[]{:S(2)}) collective-permute-start(bf16[1792,512]{1,0:T(8,128)(2,1)} %convolution_convert_fusion.5), channel_id=1, source_target_pairs={{0,4},{4,0},{8,12},{12,8},{16,20},{20,16},{24,28},{28,24},{32,36},... | collective-permute-start | bytes 5505032 | tf_op jit(solution)/shard_map/ppermute | solution.py:90
  199.8 6.9 %copy-start.20 = (bf16[448,384]{1,0:T(8,128)(2,1)S(1)}, bf16[448,384]{1,0:T(8,128)(2,1)}, u32[]{:S(2)}) copy-start(bf16[448,384]{1,0:T(8,128)(2,1)} %copy-done.19) | copy-start | bytes 1032196
  199.8 6.9 %copy-start.22 = (bf16[448,384]{1,0:T(8,128)(2,1)S(1)}, bf16[448,384]{1,0:T(8,128)(2,1)}, u32[]{:S(2)}) copy-start(bf16[448,384]{1,0:T(8,128)(2,1)} %copy-done.21) | copy-start | bytes 1032196
  199.8 6.9 %copy-start.24 = (bf16[448,384]{1,0:T(8,128)(2,1)S(1)}, bf16[448,384]{1,0:T(8,128)(2,1)}, u32[]{:S(2)}) copy-start(bf16[448,384]{1,0:T(8,128)(2,1)} %copy-done.23) | copy-start | bytes 1032196
  199.9 6.9 %copy-start.26 = (bf16[448,384]{1,0:T(8,128)(2,1)S(1)}, bf16[448,384]{1,0:T(8,128)(2,1)}, u32[]{:S(2)}) copy-start(bf16[448,384]{1,0:T(8,128)(2,1)} %copy-done.25) | copy-start | bytes 1032196
  199.9 6.9 %copy-start.35 = (bf16[384,7,128]{0,2,1:T(8,128)(2,1)S(1)}, bf16[384,7,128]{0,2,1:T(8,128)(2,1)}, u32[]{:S(2)}) copy-start(bf16[384,7,128]{0,2,1:T(8,128)(2,1)} %copy-done.34) | copy-start | bytes 2064388
  199.9 12.1 %collective-permute-start.12 = (bf16[192,896]{1,0:T(8,128)(2,1)S(1)}, bf16[192,896]{1,0:T(8,128)(2,1)S(1)}, u32[]{:S(2)}, u32[]{:S(2)}) collective-permute-start(bf16[192,896]{1,0:T(8,128)(2,1)S(1)} %get-tuple-element.10), channel_id=1, source_target_pairs={{0,1},{1,2},{2,3},{3,0},{4,5},{5,6},{6,7},{7,4},{8,9},{9,10},{10,1... | collective-permute-start | bytes 1032200 | tf_op jit(solution)/shard_map/ppermute | solution.py:89
  200.0 12.2 %collective-permute-start.14 = (bf16[192,896]{1,0:T(8,128)(2,1)S(1)}, bf16[192,896]{1,0:T(8,128)(2,1)S(1)}, u32[]{:S(2)}, u32[]{:S(2)}) collective-permute-start(bf16[192,896]{1,0:T(8,128)(2,1)S(1)} %get-tuple-element.13), channel_id=1, source_target_pairs={{0,3},{1,0},{2,1},{3,2},{4,7},{5,4},{6,5},{7,6},{8,11},{9,8},{10,9... | collective-permute-start | bytes 1032200 | tf_op jit(solution)/shard_map/ppermute | solution.py:89
  204.5 21.8 %collective-permute-start.7 = (bf16[384,896]{1,0:T(8,128)(2,1)S(1)}, bf16[384,896]{1,0:T(8,128)(2,1)S(1)}, u32[]{:S(2)}, u32[]{:S(2)}) collective-permute-start(bf16[384,896]{1,0:T(8,128)(2,1)S(1)} %pad_maximum_fusion.4), channel_id=1, source_target_pairs={{0,3},{1,0},{2,1},{3,2},{4,7},{5,4},{6,5},{7,6},{8,11},{9,8},{10,9... | collective-permute-start | bytes 2064392 | tf_op jit(solution)/shard_map/ppermute | solution.py:89
  204.7 21.7 %collective-permute-start.5 = (bf16[384,896]{1,0:T(8,128)(2,1)S(1)}, bf16[384,896]{1,0:T(8,128)(2,1)S(1)}, u32[]{:S(2)}, u32[]{:S(2)}) collective-permute-start(bf16[384,896]{1,0:T(8,128)(2,1)S(1)} %pad_maximum_fusion.3), channel_id=1, source_target_pairs={{0,1},{1,2},{2,3},{3,0},{4,5},{5,6},{6,7},{7,4},{8,9},{9,10},{10,1... | collective-permute-start | bytes 2064392 | tf_op jit(solution)/shard_map/ppermute | solution.py:89
  212.0 57.7 %collective-permute-start.16 = (bf16[1792,640]{1,0:T(8,128)(2,1)}, bf16[1792,640]{1,0:T(8,128)(2,1)}, u32[]{:S(2)}, u32[]{:S(2)}) collective-permute-start(bf16[1792,640]{1,0:T(8,128)(2,1)} %convolution_convert_fusion.3), channel_id=1, source_target_pairs={{0,4},{4,0},{8,12},{12,8},{16,20},{20,16},{24,28},{28,24},{32,36},... | collective-permute-start | bytes 6881288 | tf_op jit(solution)/shard_map/ppermute | solution.py:90
  213.3 30.3 %collective-permute-start.15 = (bf16[384,896]{1,0:T(8,128)(2,1)}, bf16[384,896]{1,0:T(8,128)(2,1)}, u32[]{:S(2)}, u32[]{:S(2)}) collective-permute-start(bf16[384,896]{1,0:T(8,128)(2,1)} %pad_maximum_fusion.7), channel_id=1, source_target_pairs={{0,3},{1,0},{2,1},{3,2},{4,7},{5,4},{6,5},{7,6},{8,11},{9,8},{10,9... | collective-permute-start | bytes 2064392 | tf_op jit(solution)/shard_map/ppermute | solution.py:89
  217.3 17.7 %copy-start.36 = (bf16[384,7,128]{0,2,1:T(8,128)(2,1)S(1)}, bf16[384,7,128]{0,2,1:T(8,128)(2,1)}, u32[]{:S(2)}) copy-start(bf16[384,7,128]{0,2,1:T(8,128)(2,1)} %copy-done.34) | copy-start | bytes 2064388
  226.3 18.3 %collective-permute-start.13 = (bf16[384,896]{1,0:T(8,128)(2,1)}, bf16[384,896]{1,0:T(8,128)(2,1)}, u32[]{:S(2)}, u32[]{:S(2)}) collective-permute-start(bf16[384,896]{1,0:T(8,128)(2,1)} %pad_maximum_fusion.6), channel_id=1, source_target_pairs={{0,1},{1,2},{2,3},{3,0},{4,5},{5,6},{6,7},{7,4},{8,9},{9,10},{10,1... | collective-permute-start | bytes 2064392 | tf_op jit(solution)/shard_map/ppermute | solution.py:89
  229.9 26.9 %all-to-all-start.1 = ((bf16[32,12,896]{2,1,0:T(8,128)(2,1)}), bf16[32,12,896]{2,1,0:T(8,128)(2,1)}, u32[]{:S(2)}, u32[]{:S(2)}) async-start(bf16[32,12,896]{2,1,0:T(8,128)(2,1)} %reshape.563), calls=%async_computation.1 | async-start | bytes 1835008 | tf_op jit(solution)/shard_map/all_to_all | solution.py:153
  240.6 22.2 %collective-permute-start.28 = (bf16[2,112,512]{2,1,0:T(8,128)(2,1)}, bf16[2,112,512]{2,1,0:T(8,128)(2,1)}, u32[]{:S(2)}, u32[]{:S(2)}) collective-permute-start(bf16[2,112,512]{2,1,0:T(8,128)(2,1)} %bitcast.105), channel_id=1, source_target_pairs={{0,24},{4,28},{8,0},{12,4},{16,8},{20,12},{24,16},{28,20},{32,56},... | collective-permute-start | bytes 688136 | tf_op jit(solution)/shard_map/ppermute | solution.py:90
  247.0 22.1 %copy-start.31 = (bf16[224,512]{1,0:T(8,128)(2,1)S(1)}, bf16[224,512]{1,0:T(8,128)(2,1)}, u32[]{:S(2)}) copy-start(bf16[224,512]{1,0:T(8,128)(2,1)} %get-tuple-element.31) | copy-start | bytes 688132
  247.0 22.2 %copy-start.30 = (bf16[224,512]{1,0:T(8,128)(2,1)S(1)}, bf16[224,512]{1,0:T(8,128)(2,1)}, u32[]{:S(2)}) copy-start(bf16[224,512]{1,0:T(8,128)(2,1)} %get-tuple-element.30) | copy-start | bytes 688132
  247.0 22.7 %copy-start.12 = (bf16[448,384]{1,0:T(8,128)(2,1)S(1)}, bf16[448,384]{1,0:T(8,128)(2,1)}, u32[]{:S(2)}) copy-start(bf16[448,384]{1,0:T(8,128)(2,1)} %copy-done.11) | copy-start | bytes 1032196
  247.0 22.7 %copy-start.14 = (bf16[448,384]{1,0:T(8,128)(2,1)S(1)}, bf16[448,384]{1,0:T(8,128)(2,1)}, u32[]{:S(2)}) copy-start(bf16[448,384]{1,0:T(8,128)(2,1)} %copy-done.13) | copy-start | bytes 1032196
  247.0 22.7 %copy-start.16 = (bf16[448,384]{1,0:T(8,128)(2,1)S(1)}, bf16[448,384]{1,0:T(8,128)(2,1)}, u32[]{:S(2)}) copy-start(bf16[448,384]{1,0:T(8,128)(2,1)} %copy-done.15) | copy-start | bytes 1032196
  247.0 22.7 %copy-start.18 = (bf16[448,384]{1,0:T(8,128)(2,1)S(1)}, bf16[448,384]{1,0:T(8,128)(2,1)}, u32[]{:S(2)}) copy-start(bf16[448,384]{1,0:T(8,128)(2,1)} %copy-done.17) | copy-start | bytes 1032196
  247.1 22.7 %copy-start.37 = (bf16[384,7,128]{0,2,1:T(8,128)(2,1)S(1)}, bf16[384,7,128]{0,2,1:T(8,128)(2,1)}, u32[]{:S(2)}) copy-start(bf16[384,7,128]{0,2,1:T(8,128)(2,1)} %copy-done.34) | copy-start | bytes 2064388
  258.2 10.9 %collective-permute-start.26 = (bf16[2,112,512]{2,1,0:T(8,128)(2,1)}, bf16[2,112,512]{2,1,0:T(8,128)(2,1)S(1)}, u32[]{:S(2)}, u32[]{:S(2)}) collective-permute-start(bf16[2,112,512]{2,1,0:T(8,128)(2,1)} %bitcast.363), channel_id=1, source_target_pairs={{0,8},{4,12},{8,16},{12,20},{16,24},{20,28},{24,0},{28,4},{32,40},... | collective-permute-start | bytes 688136 | tf_op jit(solution)/shard_map/ppermute | solution.py:90
  264.9 11.2 %collective-permute-start.29 = (bf16[4,112,512]{2,1,0:T(8,128)(2,1)S(1)}, bf16[4,112,512]{2,1,0:T(8,128)(2,1)S(1)}, u32[]{:S(2)}, u32[]{:S(2)}) collective-permute-start(bf16[4,112,512]{2,1,0:T(8,128)(2,1)S(1)} %pad_maximum_fusion.11), channel_id=1, source_target_pairs={{0,24},{4,28},{8,0},{12,4},{16,8},{20,12},{24,16},{28,20},{32,56},... | collective-permute-start | bytes 1376264 | tf_op jit(solution)/shard_map/ppermute | solution.py:90
  269.2 12.7 %collective-permute-start.27 = (bf16[4,112,512]{2,1,0:T(8,128)(2,1)S(1)}, bf16[4,112,512]{2,1,0:T(8,128)(2,1)S(1)}, u32[]{:S(2)}, u32[]{:S(2)}) collective-permute-start(bf16[4,112,512]{2,1,0:T(8,128)(2,1)S(1)} %pad_maximum_fusion.10), channel_id=1, source_target_pairs={{0,8},{4,12},{8,16},{12,20},{16,24},{20,28},{24,0},{28,4},{32,40},... | collective-permute-start | bytes 1376264 | tf_op jit(solution)/shard_map/ppermute | solution.py:90
  272.9 9.0 %slice-start = ((bf16[1792,512]{1,0:T(8,128)(2,1)}), bf16[448,512]{1,0:T(8,128)(2,1)S(1)}, s32[]{:S(2)}) async-start(bf16[1792,512]{1,0:T(8,128)(2,1)} %copy-done.7), calls=%async_computation.7 | async-start | bytes 917504 | tf_op jit(solution)/shard_map/slice | solution.py:237
  273.1 19.1 %collective-permute-start.19 = (bf16[2,112,640]{2,1,0:T(8,128)(2,1)S(1)}, bf16[2,112,640]{2,1,0:T(8,128)(2,1)S(1)}, u32[]{:S(2)}, u32[]{:S(2)}) collective-permute-start(bf16[2,112,640]{2,1,0:T(8,128)(2,1)S(1)} %bitcast.362), channel_id=1, source_target_pairs={{0,96},{4,100},{8,104},{12,108},{16,112},{20,116},{24,120},{28,124... | collective-permute-start | bytes 860168 | tf_op jit(solution)/shard_map/ppermute | solution.py:90
  275.6 16.8 %collective-permute-start.17 = (bf16[2,112,640]{2,1,0:T(8,128)(2,1)S(1)}, bf16[2,112,640]{2,1,0:T(8,128)(2,1)S(1)}, u32[]{:S(2)}, u32[]{:S(2)}) collective-permute-start(bf16[2,112,640]{2,1,0:T(8,128)(2,1)S(1)} %bitcast.361), channel_id=1, source_target_pairs={{0,32},{4,36},{8,40},{12,44},{16,48},{20,52},{24,56},{28,60},{32,6... | collective-permute-start | bytes 860168 | tf_op jit(solution)/shard_map/ppermute | solution.py:90
  282.2 6.4 %collective-permute-start.32 = (bf16[48,512]{1,0:T(8,128)(2,1)S(1)}, bf16[48,512]{1,0:T(8,128)(2,1)S(1)}, u32[]{:S(2)}, u32[]{:S(2)}) collective-permute-start(bf16[48,512]{1,0:T(8,128)(2,1)S(1)} %get-tuple-element.51), channel_id=1, source_target_pairs={{0,96},{4,100},{8,104},{12,108},{16,112},{20,116},{24,120},{28,124... | collective-permute-start | bytes 147464 | tf_op jit(solution)/shard_map/ppermute | solution.py:90
  286.8 7.9 %collective-permute-start.30 = (bf16[64,512]{1,0:T(8,128)(2,1)S(1)}, bf16[64,512]{1,0:T(8,128)(2,1)S(1)}, u32[]{:S(2)}, u32[]{:S(2)}) collective-permute-start(bf16[64,512]{1,0:T(8,128)(2,1)S(1)} %get-tuple-element.48), channel_id=1, source_target_pairs={{0,32},{4,36},{8,40},{12,44},{16,48},{20,52},{24,56},{28,60},{32,6... | collective-permute-start | bytes 196616 | tf_op jit(solution)/shard_map/ppermute | solution.py:90
  288.6 7.7 %collective-permute-start.33 = (bf16[112,512]{1,0:T(8,128)(2,1)S(1)}, bf16[112,512]{1,0:T(8,128)(2,1)S(1)}, u32[]{:S(2)}, u32[]{:S(2)}) collective-permute-start(bf16[112,512]{1,0:T(8,128)(2,1)S(1)} %pad_maximum_fusion.18), channel_id=1, source_target_pairs={{0,96},{4,100},{8,104},{12,108},{16,112},{20,116},{24,120},{28,124... | collective-permute-start | bytes 344072 | tf_op jit(solution)/shard_map/ppermute | solution.py:90
  292.3 16.1 %collective-permute-start.20 = (bf16[4,112,640]{2,1,0:T(8,128)(2,1)S(1)}, bf16[4,112,640]{2,1,0:T(8,128)(2,1)S(1)}, u32[]{:S(2)}, u32[]{:S(2)}) collective-permute-start(bf16[4,112,640]{2,1,0:T(8,128)(2,1)S(1)} %pad_maximum_fusion.9), channel_id=1, source_target_pairs={{0,96},{4,100},{8,104},{12,108},{16,112},{20,116},{24,120},{28,124... | collective-permute-start | bytes 1720328 | tf_op jit(solution)/shard_map/ppermute | solution.py:90
  292.6 15.9 %collective-permute-start.18 = (bf16[4,112,640]{2,1,0:T(8,128)(2,1)S(1)}, bf16[4,112,640]{2,1,0:T(8,128)(2,1)S(1)}, u32[]{:S(2)}, u32[]{:S(2)}) collective-permute-start(bf16[4,112,640]{2,1,0:T(8,128)(2,1)S(1)} %pad_maximum_fusion.8), channel_id=1, source_target_pairs={{0,32},{4,36},{8,40},{12,44},{16,48},{20,52},{24,56},{28,60},{32,6... | collective-permute-start | bytes 1720328 | tf_op jit(solution)/shard_map/ppermute | solution.py:90
  294.7 13.7 %collective-permute-start.31 = (bf16[112,512]{1,0:T(8,128)(2,1)S(1)}, bf16[112,512]{1,0:T(8,128)(2,1)S(1)}, u32[]{:S(2)}, u32[]{:S(2)}) collective-permute-start(bf16[112,512]{1,0:T(8,128)(2,1)S(1)} %pad_maximum_fusion.17), channel_id=1, source_target_pairs={{0,32},{4,36},{8,40},{12,44},{16,48},{20,52},{24,56},{28,60},{32,6... | collective-permute-start | bytes 344072 | tf_op jit(solution)/shard_map/ppermute | solution.py:90
  296.2 26.5 %copy-start.1 = (bf16[384,896]{1,0:T(8,128)(2,1)S(1)}, bf16[384,896]{1,0:T(8,128)(2,1)}, u32[]{:S(2)}) copy-start(bf16[384,896]{1,0:T(8,128)(2,1)} %param.9) | copy-start | bytes 2064388
  308.7 4.6 %collective-permute-start.23 = (bf16[48,640]{1,0:T(8,128)(2,1)S(1)}, bf16[48,640]{1,0:T(8,128)(2,1)S(1)}, u32[]{:S(2)}, u32[]{:S(2)}) collective-permute-start(bf16[48,640]{1,0:T(8,128)(2,1)S(1)} %get-tuple-element.47), channel_id=1, source_target_pairs={{0,24},{4,28},{8,0},{12,4},{16,8},{20,12},{24,16},{28,20},{32,56},... | collective-permute-start | bytes 184328 | tf_op jit(solution)/shard_map/ppermute | solution.py:90
  309.1 6.5 %collective-permute-start.21 = (bf16[64,640]{1,0:T(8,128)(2,1)S(1)}, bf16[64,640]{1,0:T(8,128)(2,1)S(1)}, u32[]{:S(2)}, u32[]{:S(2)}) collective-permute-start(bf16[64,640]{1,0:T(8,128)(2,1)S(1)} %get-tuple-element.44), channel_id=1, source_target_pairs={{0,8},{4,12},{8,16},{12,20},{16,24},{20,28},{24,0},{28,4},{32,40},... | collective-permute-start | bytes 245768 | tf_op jit(solution)/shard_map/ppermute | solution.py:90
  313.3 5.2 %collective-permute-start.24 = (bf16[112,640]{1,0:T(8,128)(2,1)S(1)}, bf16[112,640]{1,0:T(8,128)(2,1)S(1)}, u32[]{:S(2)}, u32[]{:S(2)}) collective-permute-start(bf16[112,640]{1,0:T(8,128)(2,1)S(1)} %pad_maximum_fusion.16), channel_id=1, source_target_pairs={{0,24},{4,28},{8,0},{12,4},{16,8},{20,12},{24,16},{28,20},{32,56},... | collective-permute-start | bytes 430088 | tf_op jit(solution)/shard_map/ppermute | solution.py:90
  315.6 6.4 %collective-permute-start.22 = (bf16[112,640]{1,0:T(8,128)(2,1)S(1)}, bf16[112,640]{1,0:T(8,128)(2,1)S(1)}, u32[]{:S(2)}, u32[]{:S(2)}) collective-permute-start(bf16[112,640]{1,0:T(8,128)(2,1)S(1)} %pad_maximum_fusion.15), channel_id=1, source_target_pairs={{0,8},{4,12},{8,16},{12,20},{16,24},{20,28},{24,0},{28,4},{32,40},... | collective-permute-start | bytes 430088 | tf_op jit(solution)/shard_map/ppermute | solution.py:90
  (19 other events, 50.8 us)
Sparse Core Ops, SparseCore 0:
  10.3 62.1 all-gather.4
  75.5 51.6 all-gather.2
  187.3 105.7 reduce-scatter.1
